TPU v7x, 32 devices: a whole 2x2x4 slice. The times are simulated.
32 devices in a mesh: px: 8 (over z, core), py: 4 (over y, x).
Axes of the slice: x: 2, y: 2, z: 4, core: 2. Of those that a mesh axis runs over, the one named last changes fastest.
Arguments:
- phase: float32 [384, 384, 384], P('px', 'py'), may hold values from -2.5 to 2.5
- material: float32 [384, 384, 384], P('px', 'py'), may hold values from 0.5 to 2
- source: float32 [384, 384, 384], P('px', 'py'), may hold values from -6 to 6
Outputs:
- phase_next: float32 [384, 384, 384], P('px', 'py')
- concentration: float32 [384, 384, 384], P('px', 'py')
All inputs are finite; a program needn't handle non-finite values.
Results may differ from a plain program's by a relative error of at most 0.00015.
Values sent between devices are 32-bit elements; how exact they have to be, the bound alone decides.
A program may use at most 256 MiB of HBM per device.

v0:
```python
import jax
import jax.numpy as jnp
from jax import lax
from jax.sharding import PartitionSpec as P

ITERS = 2


DT = 250000.0
KAPPA = 1.0
STAB = 1.0
FLOOR = 0.1
SHARP = 6.0
LEFT_VALUE = 1.0
HIGH = lax.Precision.HIGHEST


def padded_2(value, sides, width):
    for axis, dim in sides:
        peers, length = (lax.axis_size(axis), value.shape[dim])
        up = [(i, (i + 1) % peers) for i in range(peers)]
        down = [(j, i) for i, j in up]
        last = lax.slice_in_dim(value, length - width, length, axis=dim)
        leading = lax.slice_in_dim(value, 0, width, axis=dim)
        before = lax.ppermute(last, axis, up)
        after = lax.ppermute(leading, axis, down)
        value = jnp.concatenate([before, value, after], axis=dim)
    return value


def counting(length):
    return jnp.arange(length, dtype=jnp.int32)


def tables(length, rows, cols):
    product = rows[:, None] * cols[None, :] % length
    angle = 2.0 * jnp.pi / length * product.astype(jnp.float32)
    return (jnp.cos(angle), jnp.sin(angle))


def complex_table(cos_t, sin_t, sign):
    from_real = jnp.stack([cos_t, -sign * sin_t], 1)
    from_imag = jnp.stack([sign * sin_t, cos_t], 1)
    return jnp.stack([from_real, from_imag], 0)


def symbol(index, length):
    return (2.0 * jnp.sin(jnp.pi * index.astype(jnp.float32) / length)) ** 2


def filters(k_square):
    denom = 1.0 / (1.0 + DT * (KAPPA + STAB) * k_square * k_square)
    return ((1.0 + DT * STAB * k_square * k_square) * denom, -DT * k_square * denom)


def along(stacked, table, form):
    return jnp.einsum(form, stacked, table, precision=HIGH)


def body(phase, material, source):
    lx, ly, lz = phase.shape
    n_px = lax.axis_size("px")
    n_py = lax.axis_size("py")
    ix = lax.axis_index("px")
    iy = lax.axis_index("py")
    full_x = lx * n_px
    full_y = ly * n_py
    total = full_x * full_y * lz
    x_cos, x_sin = tables(full_x, counting(full_x), counting(full_x))
    y_cos, y_sin = tables(full_y, counting(full_y), counting(full_y))
    y_fwd = complex_table(y_cos, y_sin, 1.0)
    x_fwd = complex_table(x_cos, x_sin, 1.0)
    y_inv = complex_table(y_cos, y_sin, -1.0)
    x_inv = complex_table(x_cos, x_sin, -1.0)
    fields = jnp.stack([phase, phase * phase * phase - phase])
    z_cos, z_sin = tables(lz, counting(lz), counting(lz))
    spectra = jnp.einsum("fxyz,zck->cfkxy", fields, jnp.stack([z_cos, -z_sin], 1), precision=HIGH)
    spectra = lax.all_to_all(spectra, "py", split_axis=2, concat_axis=4, tiled=True)
    spectra = along(spectra, y_fwd, "cfkxy,cydq->dfkxq")
    spectra = lax.all_to_all(spectra, "px", split_axis=4, concat_axis=3, tiled=True)
    spectra = along(spectra, x_fwd, "cfkxq,cxdp->dfkqp")
    kz_loc = lz // n_py
    ky_loc = full_y // n_px
    kz_index = iy * kz_loc + counting(kz_loc)
    ky_index = ix * ky_loc + counting(ky_loc)
    plane_square = symbol(ky_index, full_y)[:, None] + symbol(counting(full_x), full_x)[None, :]
    k_square = symbol(kz_index, lz)[:, None, None] + plane_square[None]
    damp, push = filters(k_square)
    mixed = damp * spectra[:, 0] + push * spectra[:, 1]
    mixed = along(mixed, x_inv, "ckqp,cpdx->dkxq")
    mixed = lax.all_to_all(mixed, "px", split_axis=2, concat_axis=3, tiled=True)
    mixed = along(mixed, y_inv, "ckxq,cqdy->dkxy")
    mixed = lax.all_to_all(mixed, "py", split_axis=3, concat_axis=1, tiled=True)
    kz_rows = counting(lz)
    inv_cos, inv_sin = tables(lz, kz_rows, counting(lz))
    phase_next = (
        jnp.einsum("ckxy,ckz->xyz", mixed, jnp.stack([inv_cos, -inv_sin]), precision=HIGH) / total
    )
    conduct = material * (FLOOR + (1.0 - FLOOR) * jax.nn.sigmoid(SHARP * phase_next))
    padded_c = padded_2(conduct, (("px", 0), ("py", 1)), 1)
    x_pos = ix * lx + lax.broadcasted_iota(jnp.int32, (lx, 1, 1), 0)
    low_edge = x_pos == 0
    high_edge = x_pos == full_x - 1
    face_xl = jnp.where(low_edge, conduct, 0.5 * (conduct + padded_c[:-2, 1:-1]))
    face_xh = jnp.where(high_edge, conduct, 0.5 * (conduct + padded_c[2:, 1:-1]))
    face_yl = 0.5 * (conduct + padded_c[1:-1, :-2])
    face_yh = 0.5 * (conduct + padded_c[1:-1, 2:])
    face_zl = 0.5 * (conduct + jnp.roll(conduct, 1, 2))
    face_zh = 0.5 * (conduct + jnp.roll(conduct, -1, 2))
    diag = face_xl + face_xh + face_yl + face_yh + face_zl + face_zh
    weight_xl = jnp.where(low_edge, 0.0, face_xl)
    weight_xh = jnp.where(high_edge, 0.0, face_xh)

    def squares(residual):
        return lax.psum(jnp.sum(residual * residual), ("px", "py"))

    rhs = source + jnp.where(low_edge, conduct * LEFT_VALUE, 0.0)
    concentration = jnp.zeros_like(rhs)
    residual = rhs
    direction = rhs
    norm_now = squares(residual)
    for step in range(ITERS):
        padded = padded_2(direction, (("px", 0), ("py", 1)), 1)
        out = diag * direction - weight_xl * padded[:-2, 1:-1] - weight_xh * padded[2:, 1:-1]
        out = out - face_yl * padded[1:-1, :-2] - face_yh * padded[1:-1, 2:]
        image = out - face_zl * jnp.roll(direction, 1, 2) - face_zh * jnp.roll(direction, -1, 2)
        alpha = norm_now / lax.psum(jnp.sum(direction * image), ("px", "py"))
        concentration = concentration + alpha * direction
        residual = residual - alpha * image
        norm_next = squares(residual)
        direction = residual + norm_next / norm_now * direction
        norm_now = norm_next
    return (phase_next, concentration)


def solution(mesh):
    return jax.shard_map(
        body,
        mesh=mesh,
        in_specs=(P("px", "py", None), P("px", "py", None), P("px", "py", None)),
        out_specs=(P("px", "py", None), P("px", "py", None)),
        check_vma=False,
    )
```

profile of v0, /device:TPU:14, one launch (start us, length us, event | category | flops | bytes accessed | tf_op | source)
XLA Modules:
  0.0 2812.5 jit_solution(561885350023135385)
XLA Ops:
  0.6 2.4 fusion.94
  3.1 4.2 fusion.17
  7.3 48.8 %fusion.16 = f32[2,2,384,48,96]{2,4,3,1,0:T(8,128)} fusion(f32[1,48,96,384]{3,2,1,0:T(8,128)S(1)} %fusion.17, f32[1,48,96,384]{3,2,1,0:T(8,128)S(1)} %bitcast.154, f32[384,1,384]{2,0,1:T(8,128)S(1)} %get-tuple-element.42, f32[384,1,384]{2,0,1:T(8,128)S(1)} %get-tuple-element.43), kind=kOutput, calls=%fused_computation.25 | convolution fusion | flops 32618741760 | bytes 43646976 | tf_op jit(solution)/shard_map/fxyz,zck->cfkxy/dot_general | solution.py:77
  56.1 33.6 %copy.29 = f32[2,2,384,48,96]{4,3,1,0,2:T(8,128)} copy(f32[2,2,384,48,96]{2,4,3,1,0:T(8,128)} %fusion.16) | data formatting | bytes 56623104 | tf_op jit(solution)/shard_map/fxyz,zck->cfkxy/transpose | solution.py:77
  89.7 10.9 all-to-all-start
  100.6 2.3 fusion.93
  102.9 1.7 fusion.76
  104.6 401.8 %all-to-all-done = f32[2,2,384,48,96]{4,3,1,0,2:T(8,128)} async-done(((f32[2,2,384,48,96]{4,3,1,0,2:T(8,128)}), f32[2,2,384,48,96]{4,3,1,0,2:T(8,128)}, u32[]{:S(2)}, u32[]{:S(2)}) %all-to-all-start) | async-done | bytes 28311584 | tf_op jit(solution)/shard_map/all_to_all | solution.py:78
  506.4 42.5 %copy.95 = f32[2,2,4,96,48,96]{5,2,3,0,4,1:T(4,128)} copy(f32[2,2,4,96,48,96]{5,4,1,0,3,2:T(8,128)} %bitcast.14) | data formatting | bytes 56623104 | tf_op jit(solution)/shard_map/all_to_all | solution.py:78
  548.9 38.8 %reshape.206 = f32[2,2,96,48,384,1]{4,2,0,3,1,5:T(8,128)} reshape(f32[2,2,96,48,4,96]{5,4,2,0,3,1:T(4,128)} %bitcast.145) | data formatting | bytes 56623104 | tf_op jit(solution)/shard_map/all_to_all | solution.py:78
  587.7 74.2 %convolution_bitcast_fusion = f32[2,2,96,48,384]{4,2,3,1,0:T(8,128)} fusion(f32[2,2,96,48,384,1]{4,2,0,3,1,5:T(8,128)} %reshape.206, f32[1,384,2,384]{3,1,2,0:T(8,128)S(1)} %get-tuple-element.35, f32[1,384,2,384]{3,1,2,0:T(8,128)S(1)} %get-tuple-element.38), kind=kOutput, calls=%fused_computation.24 | convolution fusion | flops 65230405632 | bytes 58982400 | tf_op jit(solution)/shard_map/cfkxy,cydq->dfkxq/dot_general | solution.py:57
  661.9 33.6 %copy.32 = f32[2,2,96,48,384]{2,3,1,0,4:T(8,128)} copy(f32[2,2,96,48,384]{4,2,3,1,0:T(8,128)} %convolution_bitcast_fusion) | data formatting | bytes 56623104 | tf_op jit(solution)/shard_map/cfkxy,cydq->dfkxq/transpose | solution.py:57
  695.5 7.6 all-to-all-start.1
  703.2 0.1 broadcast_add_fusion
  703.3 6.5 fusion.19
  709.8 802.8 %all-to-all-done.1 = f32[2,2,96,48,384]{2,3,1,0,4:T(8,128)} async-done(((f32[2,2,96,48,384]{2,3,1,0,4:T(8,128)}), f32[2,2,96,48,384]{2,3,1,0,4:T(8,128)}, u32[]{:S(2)}, u32[]{:S(2)}) %all-to-all-start.1) | async-done | bytes 28311584 | tf_op jit(solution)/shard_map/all_to_all | solution.py:80
  1512.7 35.6 %copy.34 = f32[2,2,96,8,48,48]{2,5,4,3,1,0:T(8,128)} copy(f32[2,2,96,8,48,48]{2,4,1,0,5,3:T(8,128)} %bitcast.21) | data formatting | bytes 56623104 | tf_op jit(solution)/shard_map/all_to_all | solution.py:80
  1548.3 33.7 %copy.36 = f32[2,2,96,384,48]{3,2,0,4,1:T(8,128)} copy(f32[2,2,96,384,48]{2,4,3,1,0:T(8,128)} %bitcast.146) | data formatting | bytes 56623104 | tf_op jit(solution)/shard_map/all_to_all | solution.py:80
  1582.0 74.1 %fusion.13 = f32[2,2,96,48,384]{4,2,3,1,0:T(8,128)} fusion(f32[2,2,96,384,48]{3,2,0,4,1:T(8,128)} %copy.36, f32[1,384,2,384]{3,1,2,0:T(8,128)} %copy-done.8, f32[1,384,2,384]{3,1,2,0:T(8,128)} %copy-done.9), kind=kOutput, calls=%fused_computation.23 | convolution fusion | flops 65230405632 | bytes 58982400 | tf_op jit(solution)/shard_map/cfkxq,cxdp->dfkqp/dot_general | solution.py:57
  1656.2 42.2 %fusion.64 = f32[2,96,384,48]{2,1,3,0:T(8,128)} fusion(f32[2,2,96,48,384]{4,2,3,1,0:T(8,128)} %fusion.13, f32[96,48,384]{2,0,1:T(8,128)} %get-tuple-element.41, f32[96,48,384]{2,0,1:T(8,128)S(1)} %bitcast.151, f32[1,384,2,384]{3,1,2,0:T(8,128)S(1)} %copy-done.6, f32[1,384,2,384]{3,1,2,0:T(8,128)S(1)} %copy-done.4), kind=kOutput, calls=%fused_computation.114 | convolution fusion | flops 32626114560 | bytes 58982400 | tf_op jit(solution)/shard_map/ckqp,cpdx->dkxq/dot_general | solution.py:57
  1698.4 17.1 copy.40
  1715.5 418.6 %all_to_all.72 = f32[2,96,384,48]{1,3,0,2:T(8,128)} all-to-all(f32[2,96,384,48]{1,3,0,2:T(8,128)} %copy.40), channel_id=1, replica_groups=mesh['px'=8,'py'=4] {'px'}, dimensions={2} | all-to-all | bytes 28311552 | tf_op jit(solution)/shard_map/all_to_all | solution.py:91
  2134.1 7.9 copy.42
  2142.1 44.3 %fusion.67 = f32[2,96,48,384]{3,1,2,0:T(8,128)} fusion(f32[2,96,48,384,1]{1,3,2,0,4:T(8,128)S(1)} %bitcast.147, f32[1,384,2,384]{3,1,2,0:T(8,128)S(1)} %copy-done.7, f32[1,384,2,384]{3,1,2,0:T(8,128)S(1)} %copy-done.5), kind=kOutput, calls=%fused_computation.115 | convolution fusion | flops 32615497728 | bytes 30670848 | tf_op jit(solution)/shard_map/ckxq,cqdy->dkxy/dot_general | solution.py:57
  2186.4 17.2 copy.45
  2203.7 8.8 all-to-all-start.3
  2212.5 2.4 sine_negate_fusion
  2214.9 200.7 %all-to-all-done.3 = f32[2,96,48,384]{1,2,0,3:T(8,128)} async-done(((f32[2,96,48,384]{1,2,0,3:T(8,128)}), f32[2,96,48,384]{1,2,0,3:T(8,128)}, u32[]{:S(2)}, u32[]{:S(2)}) %all-to-all-start.3) | async-done | bytes 14155808 | tf_op jit(solution)/shard_map/all_to_all | solution.py:93
  2415.6 23.5 copy.96
  2439.1 19.8 all_to_all.67
  2458.9 30.3 %select_add_fusion = (f32[48,96,384]{2,1,0:T(8,128)S(1)}, f32[48,96,384]{2,1,0:T(8,128)}, f32[48,96,384]{2,1,0:T(8,128)}) fusion(f32[48,96,384]{2,1,0:T(8,128)} %param.5, pred[48]{0:T(512)(128)(4,1)S(1)} %fusion.99, f32[48,96,384]{2,1,0:T(8,128)} %param.4, f32[2,384,48,96]{1,3,0,2:T(8,128)} %all_to_all.67, f32[1,384,384]{2,1,0:T(8,128)S(1)} %get-tuple-element.46, ...), kind=kOutput, calls=%fused_computation.113 | convolution fusion | flops 16325443584 | bytes 50724912 | tf_op jit(solution)/shard_map/ckxy,ckz->xyz/dot_general | solution.py:97
  2489.2 2.9 copy-done
  2492.0 12.0 fusion.112
  2504.0 1.0 fusion.107
  2505.0 12.0 fusion.109
  2517.1 1.7 collective-permute-start.1
  2518.8 1.7 collective-permute-start.5
  2520.6 5.7 fusion.111
  2526.3 1.5 pad_maximum_fusion.37
  2527.8 1.6 collective-permute-start.2
  2529.4 0.5 collective-permute-start.3
  2529.9 0.1 pad_maximum_fusion.34
  2530.0 2.5 collective-permute-start.6
  2532.5 0.1 collective-permute-start.7
  2532.6 0.9 fusion.108
  2533.5 2.2 collective-permute-done.3
  2535.6 0.7 collective-permute-done.6
  2536.3 1.7 collective-permute-done.7
  2538.0 39.4 %multiply_reduce_fusion.1 = (f32[]{:T(128)}, f32[]{:T(128)}, f32[48,96,384]{2,1,0:T(8,128)}) fusion(f32[48,96,384]{2,1,0:T(8,128)S(1)} %bitcast.142, f32[48,96,1]{2,1,0:T(8,128)} %get-tuple-element.30, f32[48,96,383]{2,1,0:T(8,128)} %get-tuple-element.32, f32[48,96,383]{2,1,0:T(8,128)} %get-tuple-element.31, f32[48,96,1]{2,1,0:T(8,128)} %get-tuple-element.29, ...), kind=kLoop, calls=%fused_computation.110 | loop fusion | flops 102629376 | bytes 50442344 | tf_op jit(solution)/shard_map/reduce_sum | solution.py:127
  2577.3 45.8 %all-reduce = (f32[]{:T(128)}, f32[]{:T(128)}) all-reduce(f32[]{:T(128)} %get-tuple-element.3, f32[]{:T(128)} %get-tuple-element.2), channel_id=1, replica_groups=mesh['px'=8,'py'=4] {'px','py'}, use_global_device_ids=true, to_apply=%region_1.2 | all-reduce | flops 2 | bytes 16 | tf_op jit(solution)/shard_map/psum | solution.py:115
  2624.4 7.4 multiply_reduce_fusion
  2631.9 38.7 %psum.30 = f32[]{:T(128)} all-reduce(f32[]{:T(128)} %multiply_reduce_fusion), channel_id=1, replica_groups=mesh['px'=8,'py'=4] {'px','py'}, use_global_device_ids=true, to_apply=%region_5.6 | all-reduce | flops 1 | bytes 8 | tf_op jit(solution)/shard_map/psum | solution.py:115
  2671.9 6.5 multiply_add_fusion.1
  2678.3 2.9 copy-done.1
  2681.3 1.7 collective-permute-start.9
  2683.0 12.2 fusion.104
  2695.2 1.5 pad_maximum_fusion.31
  2696.7 0.5 collective-permute-start.10
  2697.3 1.5 collective-permute-start.11
  2698.8 3.0 fusion.105
  2701.8 0.9 collective-permute-done.11
  2702.7 55.6 %fusion.28 = f32[]{:T(128)} fusion(f32[48,96,384]{2,1,0:T(8,128)} %copy-done.1, f32[50,1,384]{2,1,0:T(1,128)S(1)} %collective-permute-done.11, f32[1,96,384]{2,1,0:T(8,128)S(1)} %collective-permute-done.9, f32[1,96,384]{2,1,0:T(8,128)S(1)} %collective-permute-done.8, f32[50,1,384]{2,1,0:T(1,128)S(1)} %collective-permute-done.10, ...), kind=kLoop, calls=%fused_computation.39 | loop fusion | flops 99090432 | bytes 43364452 | tf_op jit(solution)/shard_map/reduce_sum | solution.py:127
  2758.3 44.5 %psum.31 = f32[]{:T(128)} all-reduce(f32[]{:T(128)} %fusion.28), channel_id=1, replica_groups=mesh['px'=8,'py'=4] {'px','py'}, use_global_device_ids=true, to_apply=%region_7.8 | all-reduce | flops 1 | bytes 8 | tf_op jit(solution)/shard_map/psum | solution.py:127
  2804.1 8.2 multiply_add_fusion
  (56 shorter events, 0.3 us)
Async XLA Ops:
  0.6 6.6 slice-start.6
  3.0 4.2 slice-start.7
  89.7 416.7 %all-to-all-start = ((f32[2,2,384,48,96]{4,3,1,0,2:T(8,128)}), f32[2,2,384,48,96]{4,3,1,0,2:T(8,128)}, u32[]{:S(2)}, u32[]{:S(2)}) async-start(f32[2,2,384,48,96]{4,3,1,0,2:T(8,128)} %copy.29), calls=%async_computation | async-start | bytes 75497472 | tf_op jit(solution)/shard_map/all_to_all | solution.py:78
  104.6 483.1 %copy-start.8 = (f32[1,384,2,384]{3,1,2,0:T(8,128)}, f32[1,384,2,384]{3,1,2,0:T(8,128)S(1)}, u32[]{:S(2)}) copy-start(f32[1,384,2,384]{3,1,2,0:T(8,128)S(1)} %get-tuple-element.35) | copy-start | bytes 3538948
  104.6 483.1 %copy-start.9 = (f32[1,384,2,384]{3,1,2,0:T(8,128)}, f32[1,384,2,384]{3,1,2,0:T(8,128)S(1)}, u32[]{:S(2)}) copy-start(f32[1,384,2,384]{3,1,2,0:T(8,128)S(1)} %get-tuple-element.38) | copy-start | bytes 3538948
  695.5 817.2 %all-to-all-start.1 = ((f32[2,2,96,48,384]{2,3,1,0,4:T(8,128)}), f32[2,2,96,48,384]{2,3,1,0,4:T(8,128)}, u32[]{:S(2)}, u32[]{:S(2)}) async-start(f32[2,2,96,48,384]{2,3,1,0,4:T(8,128)} %copy.32), calls=%async_computation.1 | async-start | bytes 75497472 | tf_op jit(solution)/shard_map/all_to_all | solution.py:80
  1548.3 107.9 %slice-start.4 = ((s8[7077888]{0:T(1024)(128)(4,1)}), s8[2883584]{0:T(1024)(128)(4,1)S(1)}, s32[]{:S(2)}) async-start(s8[7077888]{0:T(1024)(128)(4,1)} %bitcast.150), calls=%async_computation.8 | async-start | bytes 5767168
  1582.0 74.2 %slice-start.5 = ((s8[7077888]{0:T(1024)(128)(4,1)}), s8[4194304]{0:T(1024)(128)(4,1)S(1)}, s32[]{:S(2)}) async-start(s8[7077888]{0:T(1024)(128)(4,1)} %bitcast.150), calls=%async_computation.9 | async-start | bytes 8388608
  1582.0 74.2 %copy-start.4 = (f32[1,384,2,384]{3,1,2,0:T(8,128)S(1)}, f32[1,384,2,384]{3,1,2,0:T(8,128)}, u32[]{:S(2)}) copy-start(f32[1,384,2,384]{3,1,2,0:T(8,128)} %get-tuple-element.34) | copy-start | bytes 3538948
  1582.0 74.2 %copy-start.6 = (f32[1,384,2,384]{3,1,2,0:T(8,128)S(1)}, f32[1,384,2,384]{3,1,2,0:T(8,128)}, u32[]{:S(2)}) copy-start(f32[1,384,2,384]{3,1,2,0:T(8,128)} %get-tuple-element.39) | copy-start | bytes 3538948
  2134.1 8.0 copy-start.5
  2134.1 8.0 copy-start.7
  2203.7 211.9 %all-to-all-start.3 = ((f32[2,96,48,384]{1,2,0,3:T(8,128)}), f32[2,96,48,384]{1,2,0,3:T(8,128)}, u32[]{:S(2)}, u32[]{:S(2)}) async-start(f32[2,96,48,384]{1,2,0,3:T(8,128)} %copy.45), calls=%async_computation.3 | async-start | bytes 37748736 | tf_op jit(solution)/shard_map/all_to_all | solution.py:93
  2489.1 2.9 copy-start
  2517.1 9.2 collective-permute-start
  2517.1 9.2 collective-permute-start.1
  2518.8 11.1 collective-permute-start.4
  2518.8 11.1 slice-start
  2518.8 11.1 slice-start.1
  2518.8 11.1 collective-permute-start.5
  2520.6 12.0 slice-start.2
  2526.3 6.3 slice-start.3
  2527.8 5.6 collective-permute-start.2
  2529.4 6.2 collective-permute-start.3
  2530.0 6.3 collective-permute-start.6
  2532.5 5.5 collective-permute-start.7
  2533.4 43.9 %copy-start.3 = (f32[48,96,1]{2,1,0:T(8,128)}, f32[48,96,1]{2,1,0:T(8,128)S(1)}, u32[]{:S(2)}) copy-start(f32[48,96,1]{2,1,0:T(8,128)S(1)} %get-tuple-element.24) | copy-start | bytes 55300
  2678.3 2.9 copy-start.1
  2681.2 14.0 collective-permute-start.8
  2681.3 13.9 collective-permute-start.9
  2695.2 3.6 copy-start.2
  2696.7 5.1 collective-permute-start.10
  2697.3 5.5 collective-permute-start.11
where the time goes:
time: 2820 us; the launch traced here: 2810 us
  waiting for transfers between devices  1410 us (50%)
  blocking collectives  548 us (19%)
  local copies, waits for them, and re-layouts  356 us (13%)
  matrix products  314 us (11%)
  other arithmetic  140 us (5%)
  starting transfers between devices  39.3 us (1%)
    all_to_all x1, waiting for transfers between devices, body(): lax.all_to_all(spectra, 'px', split_axis=4, concat_axis=3, tiled=True)  803 us
    all_to_all x1, blocking collectives, body(): mixed = lax.all_to_all(mixed, 'px', split_axis=2, concat_axis=3, tiled=True)  419 us
    all_to_all x1, waiting for transfers between devices, body(): lax.all_to_all(spectra, 'py', split_axis=2, concat_axis=4, tiled=True)  402 us
    dot_general x4, matrix products, along(): return jnp.einsum(form, stacked, table, precision=HIGH)  235 us
    all_to_all x1, waiting for transfers between devices, body(): mixed = lax.all_to_all(mixed, 'py', split_axis=3, concat_axis=1, tiled=True)  201 us
    reduce_sum x2, other arithmetic, body(): alpha = norm_now / lax.psum(jnp.sum(direction * image), ('px', 'py'))  95 us
    psum x2, blocking collectives, squares(): return lax.psum(jnp.sum(residual * residual), ('px', 'py'))  84.5 us
    all_to_all x2, local copies, waits for them, and re-layouts, body(): lax.all_to_all(spectra, 'py', split_axis=2, concat_axis=4, tiled=True)  81.3 us
  transfers between devices with their start and end apart: 15, of which 7 were waited for; matrix products, arithmetic and copies ran while one was open for 1% of the time, Pallas kernels for 0%

commit v1 on v0

v1 whole, which is shorter than its diff:
```python
import jax
import jax.numpy as jnp
import numpy as np
from jax import lax
from jax.sharding import PartitionSpec as P

DT = 250000.0
KAPPA = 1.0
STAB = 1.0
FLOOR = 0.1
SHARP = 6.0
LEFT_VALUE = 1.0
HIGH = lax.Precision.HIGH


def halos(value, axis, dim):
    peers, length = (lax.axis_size(axis), value.shape[dim])
    up = [(i, (i + 1) % peers) for i in range(peers)]
    down = [(j, i) for i, j in up]
    before = lax.ppermute(lax.slice_in_dim(value, length - 1, length, axis=dim), axis, up)
    after = lax.ppermute(lax.slice_in_dim(value, 0, 1, axis=dim), axis, down)
    return before, after


def neighbours(value):
    before_x, after_x = halos(value, "px", 0)
    before_y, after_y = halos(value, "py", 1)
    return (
        jnp.concatenate([before_x, value[:-1]], 0),
        jnp.concatenate([value[1:], after_x], 0),
        jnp.concatenate([before_y, value[:, :-1]], 1),
        jnp.concatenate([value[:, 1:], after_y], 1),
        jnp.roll(value, 1, 2),
        jnp.roll(value, -1, 2),
    )


def angles(length, rows, cols):
    product = np.arange(rows)[:, None] * np.arange(cols)[None, :] % length
    angle = 2.0 * np.pi / length * product
    return np.cos(angle), np.sin(angle)


def complex_table(length, sign):
    cos_t, sin_t = angles(length, length, length)
    real = np.stack([cos_t, sign * sin_t], -1)
    imag = np.stack([-sign * sin_t, cos_t], -1)
    return np.stack([real, imag], 1).astype(np.float32)


def symbol(length, count):
    return ((2.0 * np.sin(np.pi * np.arange(count) / length)) ** 2).astype(np.float32)


def exchange(value, axis):
    return lax.all_to_all(value, axis, split_axis=0, concat_axis=0, tiled=True)


def body(phase, material, source):
    lx, ly, lz = phase.shape
    n_px = lax.axis_size("px")
    n_py = lax.axis_size("py")
    ix = lax.axis_index("px")
    iy = lax.axis_index("py")
    full_x = lx * n_px
    full_y = ly * n_py
    total = full_x * full_y * lz
    half = lz // 2 + 1
    kz_loc = -(-half // n_py)
    kz_all = kz_loc * n_py
    ky_loc = full_y // n_px
    cos_z, sin_z = angles(lz, kz_all, lz)
    rows = np.arange(kz_all)
    held = (rows < half).astype(np.float64)[:, None]
    twice = np.where((rows == 0) | (2 * rows == lz), 1.0, 2.0)[:, None] * held / total
    z_fwd = np.stack([cos_z * held, -sin_z * held]).reshape(2, n_py, kz_loc, lz).astype(np.float32)
    z_inv = np.stack([cos_z * twice, -sin_z * twice]).reshape(2, n_py, kz_loc, lz).astype(np.float32)

    fields = jnp.stack([phase, phase * phase * phase - phase])
    spectra = jnp.einsum("fxyz,cpkz->pycfxk", fields, z_fwd, precision=HIGH)
    spectra = exchange(spectra.reshape(n_py, ly, 2, 2, lx * kz_loc), "py")
    spectra = spectra.reshape(full_y, 2, 2, lx * kz_loc)
    spectra = jnp.einsum("qdyc,ycfm->qdfm", complex_table(full_y, 1.0), spectra, precision=HIGH)
    spectra = spectra.reshape(n_px, ky_loc, 2, 2, lx, kz_loc).transpose(0, 4, 2, 3, 1, 5)
    spectra = exchange(spectra.reshape(n_px, lx, 2, 2, ky_loc * kz_loc), "px")
    spectra = spectra.reshape(full_x, 2, 2, ky_loc * kz_loc)
    spectra = jnp.einsum("pdxc,xcfm->fpdm", complex_table(full_x, 1.0), spectra, precision=HIGH)

    y_part = lax.dynamic_slice_in_dim(jnp.asarray(symbol(full_y, full_y)), ix * ky_loc, ky_loc)
    z_part = lax.dynamic_slice_in_dim(jnp.asarray(symbol(lz, kz_all)), iy * kz_loc, kz_loc)
    plane = (y_part[:, None] + z_part[None, :]).reshape(-1)
    k_square = symbol(full_x, full_x)[:, None, None] + plane[None, None, :]
    denom = 1.0 / (1.0 + DT * (KAPPA + STAB) * k_square * k_square)
    damp = (1.0 + DT * STAB * k_square * k_square) * denom
    push = -DT * k_square * denom
    mixed = damp * spectra[0] + push * spectra[1]

    mixed = jnp.einsum("xdpc,pcm->xdm", complex_table(full_x, -1.0), mixed, precision=HIGH)
    mixed = exchange(mixed.reshape(n_px, lx, 2, ky_loc * kz_loc), "px")
    mixed = mixed.reshape(n_px, lx, 2, ky_loc, kz_loc).transpose(0, 3, 2, 1, 4)
    mixed = mixed.reshape(full_y, 2, lx * kz_loc)
    mixed = jnp.einsum("ydqc,qcm->ydm", complex_table(full_y, -1.0), mixed, precision=HIGH)
    mixed = exchange(mixed.reshape(n_py, ly, 2, lx * kz_loc), "py")
    mixed = mixed.reshape(n_py, ly, 2, lx, kz_loc)
    phase_next = jnp.einsum("pycxk,cpkz->xyz", mixed, z_inv, precision=HIGH)

    conduct = material * (FLOOR + (1.0 - FLOOR) * jax.nn.sigmoid(SHARP * phase_next))
    near = neighbours(conduct)
    x_pos = ix * lx + lax.broadcasted_iota(jnp.int32, (lx, 1, 1), 0)
    low_edge = x_pos == 0
    high_edge = x_pos == full_x - 1
    face_xl = jnp.where(low_edge, conduct, 0.5 * (conduct + near[0]))
    face_xh = jnp.where(high_edge, conduct, 0.5 * (conduct + near[1]))
    face_yl, face_yh, face_zl, face_zh = [0.5 * (conduct + other) for other in near[2:]]
    diag = face_xl + face_xh + face_yl + face_yh + face_zl + face_zh
    weight_xl = jnp.where(low_edge, 0.0, face_xl)
    weight_xh = jnp.where(high_edge, 0.0, face_xh)

    def operate(field):
        xl, xh, yl, yh, zl, zh = neighbours(field)
        out = diag * field - weight_xl * xl - weight_xh * xh
        out = out - face_yl * yl - face_yh * yh
        return out - face_zl * zl - face_zh * zh

    def sums(*pairs):
        return lax.psum(jnp.stack([jnp.sum(a * b) for a, b in pairs]), ("px", "py"))

    rhs = source + jnp.where(low_edge, conduct * LEFT_VALUE, 0.0)
    image = operate(rhs)
    norm_now, curve = sums((rhs, rhs), (rhs, image))
    alpha = norm_now / curve
    residual = rhs - alpha * image
    image_r = operate(residual)
    norm_next, curve_r, cross = sums((residual, residual), (residual, image_r), (residual, image))
    beta = norm_next / norm_now
    alpha_2 = norm_next / (curve_r + 2.0 * beta * cross + beta * beta * curve)
    concentration = (alpha + alpha_2 * beta) * rhs + alpha_2 * residual
    return (phase_next, concentration)


def solution(mesh):
    return jax.shard_map(
        body,
        mesh=mesh,
        in_specs=(P("px", "py", None), P("px", "py", None), P("px", "py", None)),
        out_specs=(P("px", "py", None), P("px", "py", None)),
        check_vma=False,
    )
```

time: 2820 us -> 1520 us (0.54)
  waiting for transfers between devices: 1410 us -> 398 us
  matrix products: 314 us -> 141 us
  blocking collectives: 548 us -> 428 us
  local copies, waits for them, and re-layouts: 356 us -> 407 us
  other arithmetic: 140 us -> 100 us
    all_to_all x3 -> x2, waiting for transfers between devices: 1410 us -> 398 us  [exchange(): return lax.all_to_all(value, axis, split_axis=0, concat_axis=0, tiled=True)]
    dot_general x6, matrix products: 314 us -> 141 us  [the longest x1 42.7 us: body(): jnp.einsum('pdxc,xcfm->fpdm', complex_table(full_x, 1.0), spectra, precis...]
    reshape x0 -> x9, local copies, waits for them, and re-layouts: none -> 167 us  [the longest x2 35.7 us: body(): mixed = mixed.reshape(n_px, lx, 2, ky_loc, kz_loc).transpose(0, 3, 2, 1, 4)]
    all_to_all x7 -> x3, local copies, waits for them, and re-layouts: 202 us -> 37.2 us  [exchange(): return lax.all_to_all(value, axis, split_axis=0, concat_axis=0, tiled=True)]
    all_to_all x1 -> x2, blocking collectives: 419 us -> 342 us  [exchange(): return lax.all_to_all(value, axis, split_axis=0, concat_axis=0, tiled=True)]
    slice x9 -> x14, local copies, waits for them, and re-layouts: 46.8 us -> 114 us  [the longest x4 45.8 us: neighbours(): jnp.roll(value, 1, 2)]
    psum x3 -> x2, blocking collectives: 129 us -> 86.5 us  [sums(): return lax.psum(jnp.stack([jnp.sum(a * b) for a, b in pairs]), ('px', 'py'))]
    transpose x4 -> x2, local copies, waits for them, and re-layouts: 102 us -> 69.9 us  [the longest x1 35.8 us: body(): spectra.reshape(n_px, ky_loc, 2, 2, lx, kz_loc).transpose(0, 4, 2, 3, 1, 5)]
  transfers between devices with their start and end apart: 15 -> 14, of which waited for: 7 -> 2; matrix products, arithmetic and copies ran while one was open for 1% -> 1% of each run, Pallas kernels for 0% -> 0%
where the time goes in v1:
time: 1520 us; the launch traced here: 1510 us
  blocking collectives  428 us (28%)
  local copies, waits for them, and re-layouts  407 us (27%)
  waiting for transfers between devices  398 us (26%)
  matrix products  141 us (9%)
  other arithmetic  100 us (7%)
  starting transfers between devices  25.9 us (2%)
    all_to_all x2, waiting for transfers between devices, exchange(): return lax.all_to_all(value, axis, split_axis=0, concat_axis=0, tiled=True)  398 us
    all_to_all x2, blocking collectives, exchange(): return lax.all_to_all(value, axis, split_axis=0, concat_axis=0, tiled=True)  342 us
    psum x2, blocking collectives, sums(): return lax.psum(jnp.stack([jnp.sum(a * b) for a, b in pairs]), ('px', 'py'))  86.5 us
    reduce_sum x3, other arithmetic, sums(): return lax.psum(jnp.stack([jnp.sum(a * b) for a, b in pairs]), ('px', 'py'))  82.7 us
    slice x4, local copies, waits for them, and re-layouts, neighbours(): jnp.roll(value, 1, 2)  45.8 us
    dot_general x1, matrix products, body(): jnp.einsum('pdxc,xcfm->fpdm', complex_table(full_x, 1.0), spectra, precis...  42.7 us
    all_to_all x3, local copies, waits for them, and re-layouts, exchange(): return lax.all_to_all(value, axis, split_axis=0, concat_axis=0, tiled=True)  37.2 us
    transpose x1, local copies, waits for them, and re-layouts, body(): spectra.reshape(n_px, ky_loc, 2, 2, lx, kz_loc).transpose(0, 4, 2, 3, 1, 5)  35.8 us
  transfers between devices with their start and end apart: 14, of which 2 were waited for; matrix products, arithmetic and copies ran while one was open for 1% of the time, Pallas kernels for 0%

profile of v1, /device:TPU:14, one launch (start us, length us, event | category | flops | bytes accessed | tf_op | source)
XLA Modules:
  0.0 1506.8 jit_solution(16491435841998416959)
XLA Ops:
  0.7 4.2 fusion.18
  4.8 1.0 copy-done.3
  5.9 20.9 %fusion.8 = f32[4,96,2,2,48,49]{1,5,0,2,4,3:T(8,128)} fusion(f32[2,4,49,384,1,1]{3,2,1,0,5,4:T(8,128)S(1)} %copy-done.6, f32[1,48,96,384]{3,2,1,0:T(8,128)S(1)} %fusion.18, f32[1,48,96,384]{3,2,1,0:T(8,128)S(1)} %bitcast.116), kind=kOutput, calls=%fused_computation.15 | convolution fusion | flops 8327135232 | bytes 29208576 | tf_op jit(solution)/shard_map/fxyz,cpkz->pycfxk/dot_general | solution.py:80
  26.8 34.1 %copy.37 = f32[4,96,2,2,48,49]{1,3,5,4,2,0:T(2,128)} copy(f32[4,96,2,2,48,49]{1,5,0,2,4,3:T(8,128)} %fusion.8) | data formatting | bytes 28901376 | tf_op jit(solution)/shard_map/fxyz,cpkz->pycfxk/transpose | solution.py:80
  61.0 26.0 %copy.38 = f32[4,96,2,2,2352]{4,1,3,2,0:T(8,128)} copy(f32[4,96,2,2,2352]{1,3,4,2,0:T(2,128)} %bitcast.112) | data formatting | bytes 28901376 | tf_op jit(solution)/shard_map/reshape | solution.py:81
  87.0 172.2 %all_to_all.20 = f32[4,96,2,2,2352]{4,1,3,2,0:T(8,128)} all-to-all(f32[4,96,2,2,2352]{4,1,3,2,0:T(8,128)} %copy.38), channel_id=1, replica_groups=mesh['px'=8,'py'=4] {'py'}, dimensions={0} | all-to-all | bytes 28901376 | tf_op jit(solution)/shard_map/all_to_all | solution.py:56
  259.2 11.8 copy.39
  271.0 24.9 %convolution_bitcast_fusion = f32[384,2,2,2352]{3,0,2,1:T(8,128)} fusion(f32[384,2,2,2352,1]{3,0,2,1,4:T(8,128)} %bitcast.110, f32[384,2,384,2,1]{2,0,3,4,1:T(8,128)S(1)} %copy-done.2), kind=kOutput, calls=%fused_computation.13 | convolution fusion | flops 16647192576 | bytes 31260672 | tf_op jit(solution)/shard_map/qdyc,ycfm->qdfm/dot_general | solution.py:83
  295.9 34.4 %reshape.138 = f32[8,48,2,2,48,49]{5,4,1,0,3,2:T(8,128)} reshape(f32[384,2,2,2352]{3,0,2,1:T(8,128)} %convolution_bitcast_fusion) | data formatting | bytes 28901376 | tf_op jit(solution)/shard_map/reshape | solution.py:84
  330.4 35.8 %copy.42 = f32[8,48,2,2,48,49]{5,4,1,3,2,0:T(8,128)} copy(f32[8,48,2,2,48,49]{5,1,4,0,3,2:T(8,128)} %bitcast.111) | data formatting | bytes 28901376 | tf_op jit(solution)/shard_map/transpose | solution.py:84
  366.2 29.8 %reshape.139 = f32[8,48,2,2,2352]{4,1,3,2,0:T(8,128)} reshape(f32[8,48,2,2,48,49]{5,4,1,3,2,0:T(8,128)} %copy.42) | data formatting | bytes 28901376 | tf_op jit(solution)/shard_map/reshape | solution.py:85
  395.9 5.7 all-to-all-start.1
  401.9 0.1 add.153
  402.0 3.8 fusion.42
  405.8 316.6 %all-to-all-done.1 = f32[8,48,2,2,2352]{4,1,3,2,0:T(8,128)} async-done(((f32[8,48,2,2,2352]{4,1,3,2,0:T(8,128)}), f32[8,48,2,2,2352]{4,1,3,2,0:T(8,128)}, u32[]{:S(2)}, u32[]{:S(2)}) %all-to-all-start.1) | async-done | bytes 14450720 | tf_op jit(solution)/shard_map/all_to_all | solution.py:56
  722.4 11.9 copy.43
  734.3 42.7 %fusion.5 = f32[2,384,2,2352]{1,3,2,0:T(8,128)} fusion(f32[384,2,384,2,1]{2,0,3,1,4:T(8,128)} %constant.67, f32[384,2,2,2352,1]{3,0,2,1,4:T(8,128)} %bitcast.117), kind=kOutput, calls=%fused_computation.14 | convolution fusion | flops 16647192576 | bytes 31260672 | tf_op jit(solution)/shard_map/pdxc,xcfm->fpdm/dot_general | solution.py:87
  777.0 15.3 %fusion.14 = f32[384,2,2352,1]{2,0,3,1:T(8,128)S(1)} fusion(f32[384,2,384,2]{2,0,3,1:T(8,128)} %constant.62.clone, f32[2,384,2,2352]{1,3,2,0:T(8,128)} %fusion.5, f32[384,2352]{0,1:T(8,128)} %get-tuple-element.53, f32[384,2352]{0,1:T(8,128)S(1)} %copy-done.4), kind=kOutput, calls=%fused_computation.22 | convolution fusion | flops 8329015296 | bytes 31260672 | tf_op jit(solution)/shard_map/xdpc,pcm->xdm/dot_general | solution.py:98
  792.3 0.5 copy.46
  792.9 169.6 %all_to_all.21 = f32[8,48,2,2352]{3,1,2,0:T(8,128)} all-to-all(f32[8,48,2,2352]{3,1,2,0:T(8,128)S(1)} %copy.46), channel_id=1, replica_groups=mesh['px'=8,'py'=4] {'px'}, dimensions={0} | all-to-all | bytes 14450688 | tf_op jit(solution)/shard_map/all_to_all | solution.py:56
  962.5 18.1 %reshape.142 = f32[8,48,2,48,49]{4,3,1,2,0:T(8,128)} reshape(f32[8,48,2,2352]{3,1,2,0:T(8,128)} %all_to_all.21) | data formatting | bytes 14450688 | tf_op jit(solution)/shard_map/reshape | solution.py:100
  980.6 17.6 %copy.84 = f32[8,48,2,48,49]{4,1,3,0,2:T(8,128)} copy(f32[8,48,2,48,49]{4,3,1,2,0:T(8,128)} %reshape.142) | data formatting | bytes 14450688 | tf_op jit(solution)/shard_map/reshape | solution.py:100
  998.3 15.8 %reshape.143 = f32[384,2,2352]{2,0,1:T(8,128)} reshape(f32[8,48,2,48,49]{4,3,1,0,2:T(8,128)} %bitcast.113) | data formatting | bytes 14450688 | tf_op jit(solution)/shard_map/reshape | solution.py:101
  1014.1 12.5 fusion.9
  1026.6 3.5 copy.50
  1030.1 8.1 all-to-all-start.3
  1038.3 81.1 %all-to-all-done.3 = f32[4,96,2,2352]{3,1,2,0:T(8,128)} async-done(((f32[4,96,2,2352]{3,1,2,0:T(8,128)}), f32[4,96,2,2352]{3,1,2,0:T(8,128)}, u32[]{:S(2)}, u32[]{:S(2)}) %all-to-all-start.3) | async-done | bytes 7225376 | tf_op jit(solution)/shard_map/all_to_all | solution.py:56
  1119.4 13.6 copy.51
  1132.9 21.4 %copy.52 = f32[4,96,2,48,49]{4,3,0,2,1:T(8,128)} copy(f32[4,96,2,48,49]{1,2,4,3,0:T(2,128)} %bitcast.114) | data formatting | bytes 14450688 | tf_op jit(solution)/shard_map/reshape | solution.py:104
  1154.3 25.2 %copy_add_fusion = (f32[48,96,384]{2,0,1:T(8,128)S(1)}, f32[48,96,384]{2,0,1:T(8,128)}, f32[48,96,384]{2,0,1:T(8,128)}) fusion(f32[48,96,384]{2,1,0:T(8,128)} %param.14, pred[48]{0:T(512)(128)(4,1)S(1)} %fusion.50, f32[48,96,384]{2,1,0:T(8,128)} %param.13, f32[4,96,2,48,49]{4,3,0,2,1:T(8,128)} %copy.52, f32[2,4,49,384,1]{3,2,1,0,4:T(8,128)S(1)} %copy-done.8), kind=kOutput, calls=%fused_computation.65 | convolution fusion | flops 4177723392 | bytes 43216944 | tf_op jit(solution)/shard_map/pycxk,cpkz->xyz/dot_general | solution.py:105
  1179.5 1.1 fusion.61
  1180.6 3.3 fusion.59
  1183.9 0.6 fusion.67
  1184.5 20.0 %fusion.62 = (f32[48,95,384]{2,0,1:T(8,128)}, f32[48,95,384]{2,0,1:T(8,128)}, f32[48,95,384]{2,0,1:T(8,128)}, f32[48,95,384]{2,0,1:T(8,128)}) fusion(f32[48,96,384]{2,0,1:T(8,128)} %get-tuple-element.15, f32[48,96,384]{2,0,1:T(8,128)} %copy-done), kind=kLoop, calls=%fused_computation.100 | loop fusion | bytes 56033280 | tf_op jit(solution)/shard_map/slice | solution.py:31
  1204.5 20.5 %fusion.64 = (f32[48,96,383]{2,0,1:T(8,128)}, f32[48,96,383]{2,0,1:T(8,128)}, f32[48,96,383]{2,0,1:T(8,128)}, f32[48,96,383]{2,0,1:T(8,128)}) fusion(f32[48,96,384]{2,0,1:T(8,128)} %get-tuple-element.15, f32[48,96,384]{2,0,1:T(8,128)} %copy-done), kind=kLoop, calls=%fused_computation.102 | loop fusion | bytes 56475648 | tf_op jit(solution)/shard_map/jit(_roll_static)/slice | solution.py:33
  1225.0 18.7 %fusion.60 = (f32[47,96,384]{2,0,1:T(8,128)}, f32[47,96,384]{2,0,1:T(8,128)}, f32[47,96,384]{2,0,1:T(8,128)}, f32[47,96,384]{2,0,1:T(8,128)}) fusion(f32[48,96,384]{2,0,1:T(8,128)} %get-tuple-element.15, f32[48,96,384]{2,0,1:T(8,128)} %copy-done), kind=kLoop, calls=%fused_computation.98 | loop fusion | bytes 55443456 | tf_op jit(solution)/shard_map/slice | solution.py:29
  1243.7 1.5 collective-permute-start.2
  1245.2 0.5 collective-permute-start.3
  1245.7 2.5 collective-permute-start.6
  1248.3 1.8 fusion.65
  1250.2 1.7 collective-permute-start.1
  1252.0 1.7 collective-permute-start.5
  1253.7 8.0 fusion.63
  1261.8 39.5 %multiply_reduce_fusion.3 = (f32[]{:T(128)}, f32[]{:T(128)}, f32[48,96,384]{2,0,1:T(8,128)}) fusion(f32[48,96,384]{2,0,1:T(8,128)} %copy-done, f32[48,96,1]{2,0,1:T(8,128)} %get-tuple-element.64, f32[48,96,383]{2,0,1:T(8,128)} %get-tuple-element.66, f32[48,96,383]{2,0,1:T(8,128)} %get-tuple-element.67, f32[48,96,1]{2,0,1:T(8,128)} %get-tuple-element.65, ...), kind=kLoop, calls=%fused_computation.73 | loop fusion | flops 88473600 | bytes 106168424 | tf_op jit(solution)/shard_map/reduce_sum | solution.py:126
  1301.3 1.4 pad_maximum_fusion
  1302.6 46.2 %psum.14 = f32[2]{0:T(128)S(1)} all-reduce(f32[2]{0:T(128)S(1)} %pad_maximum_fusion), channel_id=1, replica_groups=mesh['px'=8,'py'=4] {'px','py'}, use_global_device_ids=true, to_apply=%region_2.3 | all-reduce | flops 2 | bytes 16 | tf_op jit(solution)/shard_map/psum | solution.py:126
  1348.9 0.6 fusion.72
  1350.8 6.8 multiply_reduce_fusion.1
  1357.6 0.7 fusion.55
  1358.3 2.3 copy-done.1
  1360.6 0.2 fusion.53
  1360.8 10.9 fusion.56
  1371.7 12.0 fusion.58
  1383.7 11.1 fusion.54
  1394.9 2.0 collective-permute-start.11
  1396.9 1.9 collective-permute-start.9
  1398.8 5.3 fusion.57
  1404.1 36.4 %fusion.40 = f32[]{:T(128)} fusion(f32[48,96,384]{2,0,1:T(8,128)} %copy-done.1, f32[48,96,1]{2,0,1:T(8,128)} %get-tuple-element.25, f32[48,96,383]{2,0,1:T(8,128)} %get-tuple-element.27, f32[48,96,383]{2,0,1:T(8,128)} %get-tuple-element.26, f32[48,96,1]{2,0,1:T(8,128)} %get-tuple-element.24, f32[48,1,384]{2,0,1:T(8,128)S(1)} %collective-permute-done.11, ...), kind=kLoop, calls=%fused_computation.74 | loop fusion | flops 84934656 | bytes 99090528 | tf_op jit(solution)/shard_map/reduce_sum | solution.py:126
  1440.6 1.9 pad_maximum_fusion.1
  1442.4 8.2 copy.55
  1450.7 40.3 %psum.15 = f32[3]{0:T(128)S(1)} all-reduce(f32[3]{0:T(128)S(1)} %pad_maximum_fusion.1), channel_id=1, replica_groups=mesh['px'=8,'py'=4] {'px','py'}, use_global_device_ids=true, to_apply=%region_6.7 | all-reduce | flops 3 | bytes 24 | tf_op jit(solution)/shard_map/psum | solution.py:126
  1491.0 0.6 fusion.71
  1495.6 5.9 multiply_add_fusion
  1501.5 5.1 copy.56
  (40 shorter events, 0.4 us)
Async XLA Ops:
  0.6 4.2 copy-start.6
  0.6 5.2 copy-start.3
  259.2 11.8 copy-start.2
  395.9 5.7 copy-start.7
  395.9 5.8 copy-start.9
  395.9 326.5 %all-to-all-start.1 = ((f32[8,48,2,2,2352]{4,1,3,2,0:T(8,128)}), f32[8,48,2,2,2352]{4,1,3,2,0:T(8,128)}, u32[]{:S(2)}, u32[]{:S(2)}) async-start(f32[8,48,2,2,2352]{4,1,3,2,0:T(8,128)} %reshape.139), calls=%async_computation.1 | async-start | bytes 29884416 | tf_op jit(solution)/shard_map/all_to_all | solution.py:56
  734.3 42.7 %copy-start.4 = (f32[384,2352]{0,1:T(8,128)S(1)}, f32[384,2352]{0,1:T(8,128)}, u32[]{:S(2)}) copy-start(f32[384,2352]{0,1:T(8,128)} %get-tuple-element.52) | copy-start | bytes 10838020
  998.2 15.8 %copy-start.5 = (f32[384,2,384,2]{2,0,3,1:T(8,128)S(1)}, f32[384,2,384,2]{2,0,3,1:T(8,128)}, u32[]{:S(2)}) copy-start(f32[384,2,384,2]{2,0,3,1:T(8,128)} %constant.62.clone) | copy-start | bytes 7077892
  1030.1 89.2 %all-to-all-start.3 = ((f32[4,96,2,2352]{3,1,2,0:T(8,128)}), f32[4,96,2,2352]{3,1,2,0:T(8,128)}, u32[]{:S(2)}, u32[]{:S(2)}) async-start(f32[4,96,2,2352]{3,1,2,0:T(8,128)} %copy.50), calls=%async_computation.3 | async-start | bytes 14942208 | tf_op jit(solution)/shard_map/all_to_all | solution.py:56
  1132.9 21.4 %copy-start.8 = (f32[2,4,49,384,1]{3,2,1,0,4:T(8,128)S(1)}, f32[2,4,49,384,1]{3,2,1,0,4:T(8,128)}, u32[]{:S(2)}) copy-start(f32[2,4,49,384,1]{3,2,1,0,4:T(8,128)} %constant.68) | copy-start | bytes 1806340
  1179.5 4.4 copy-start
  1243.7 6.5 collective-permute-start.2
  1245.2 6.8 collective-permute-start.3
  1245.7 6.2 collective-permute-start.6
  1250.1 11.6 collective-permute-start.7
  1250.2 11.6 collective-permute-start
  1250.2 11.5 collective-permute-start.1
  1252.0 9.8 collective-permute-start.4
  1252.0 9.8 collective-permute-start.5
  1357.6 3.0 copy-start.1
  1394.9 9.2 collective-permute-start.10
  1394.9 9.2 collective-permute-start.11
  1396.9 7.2 collective-permute-start.8
  1396.9 7.2 collective-permute-start.9
